TPU v7x, 32 devices: a whole 2x2x4 slice. The times are simulated.
32 devices in a mesh: dom: 8 (over z, core), sub: 4 (over y, x).
Axes of the slice: x: 2, y: 2, z: 4, core: 2. Of those that a mesh axis runs over, the one named last changes fastest.
Arguments:
- state: bfloat16 [32768, 256], P(('dom', 'sub')), may hold values from -6 to 6
- tile_values: float32 [32, 24, 128, 128], P(('dom', 'sub')), may hold values from 0.0003125 to 0.009375
- tile_rows: int32 [32, 24], P(('dom', 'sub')), may hold values from 0 to 7, as said below
- tile_columns: int32 [32, 24], P(('dom', 'sub')), may hold values from 0 to 7, as said below
- tile_counts: int32 [32], P(('dom', 'sub')), may hold values from 8 to 24, as said below
- send_nodes: int32 [32, 4, 256], P(('dom', 'sub')), may hold values from 0 to 1023
- face_counts: int32 [32, 4], P(('dom', 'sub')), may hold values from 0 to 256, as said below
- capacity: float32 [32768], P(('dom', 'sub')), may hold values from 0.05 to 2
- source: float32 [32768], P(('dom', 'sub')), may hold values from -12 to 12
- w_self: bfloat16 [2, 256, 256], replicated, may hold values from -0.375 to 0.375
- w_neighbour: bfloat16 [2, 256, 256], replicated, may hold values from -0.375 to 0.375
- w_out: bfloat16 [2, 256, 256], replicated, may hold values from -0.375 to 0.375
- gains: float32 [2, 2, 256], replicated, may hold values from 0.25 to 1.75
- bias: float32 [2, 256], replicated, may hold values from -3 to 3
- w_decode: float32 [256], replicated, may hold values from -0.375 to 0.375
Outputs:
- heat_level_field: float32 [32768], P(('dom', 'sub'))
- equation_defect: float32 [32768], P(('dom', 'sub'))
Inputs may be any that keep to these rules, and one draw needn't show every extreme that they name: `tile_counts`: slots at or beyond a device's count are ignored; some device has all 24 slots live. `tile_rows`: slot t < 8 names tile t, in tile_columns as well. `tile_columns`: slot t < 8 names tile t, in tile_rows as well. `face_counts`: two neighbouring devices give each other the same count; the count is 0 toward a side where the slice has no neighbour; some pair of neighbours fills all 256 slots.
All inputs are finite; a program needn't handle non-finite values.
Results may differ from a plain program's by a relative error of at most 0.005.
Values may be sent and summed in bfloat16 or wider, within the bound.
No kernel may reach another device: no remote copies, remote signals or barrier semaphores. Data moves between devices by JAX's collectives and lax.ppermute only.
A program may use at most 64 MiB of HBM per device.

v0:
```python
import functools

import jax
import jax.numpy as jnp
from jax import lax
from jax.experimental import pallas as pl
from jax.experimental.pallas import tpu as pltpu
from jax.sharding import PartitionSpec as P

LAYERS = 2
ITERS = 3
LANES = 128
MATCHINGS = ((1, 1), (1, 0), (0, 0), (0, 1))
VMEM_LIMIT = 24 * 1024 * 1024

F32 = jnp.float32
BF16 = jnp.bfloat16


def shape(dims, dtype=F32):
    return jax.ShapeDtypeStruct(dims, dtype)


def run(body, outs, operands, scalars=(), raw=(), scratch=(), waits=0, flops=1_000_000, moved=1_000_000):
    smem = pl.BlockSpec(memory_space=pltpu.SMEM)
    vmem = pl.BlockSpec(memory_space=pltpu.VMEM)
    anywhere = pl.BlockSpec(memory_space=pltpu.HBM)
    scratch = list(scratch) + [pltpu.SemaphoreType.DMA((waits,))] * bool(waits)
    return pl.pallas_call(
        body,
        out_shape=outs,
        in_specs=[smem] * len(scalars) + [vmem] * len(operands) + [anywhere] * len(raw),
        out_specs=[vmem] * len(outs),
        scratch_shapes=scratch,
        compiler_params=pltpu.CompilerParams(vmem_limit_bytes=VMEM_LIMIT),
        cost_estimate=pl.CostEstimate(flops=flops, bytes_accessed=moved, transcendentals=0),
    )(*scalars, *operands, *(pltpu.with_memory_space_constraint(r, pltpu.HBM) for r in raw))


def copies(pairs, semaphores):
    started = [pltpu.make_async_copy(*pair, semaphores.at[i]) for i, pair in enumerate(pairs)]
    for copy in started:
        copy.start()
    return started


def slot_rows(places):
    return [places[r : r + 1, :] for r in range(places.shape[0])]


def pick(vector, rows):
    index = jnp.concatenate(rows, axis=0)
    low = jnp.bitwise_and(index, LANES - 1)
    high = jnp.right_shift(index, 7)
    out = jnp.zeros(index.shape, F32)
    for t in range(vector.shape[0]):
        spread = jnp.broadcast_to(vector[t : t + 1, :], index.shape)
        got = jnp.take_along_axis(spread, low, axis=1, mode="promise_in_bounds")
        out = jnp.where(high == t, got, out)
    return out


def pieces(value):
    first = value.astype(BF16)
    rest = value - first.astype(F32)
    second = rest.astype(BF16)
    third = (rest - second.astype(F32)).astype(BF16)
    return first, second, third


def low_hits(rows):
    lane = lax.broadcasted_iota(jnp.int32, (LANES, LANES), 0)
    return jnp.concatenate(
        [(lane == jnp.bitwise_and(row, LANES - 1)).astype(F32).astype(BF16) for row in rows], axis=1
    )


def spread_sum(values, rows, tiles):
    tile = lax.broadcasted_iota(jnp.int32, (tiles, LANES), 0)
    parts = [
        jnp.where(tile == jnp.right_shift(row, 7), value, 0.0) for value, row in zip(values, rows)
    ]
    held = jnp.concatenate(parts, axis=1)
    stacked = jnp.concatenate([p.astype(F32) for p in pieces(held)], axis=0).astype(BF16)
    out = lax.dot_general(
        stacked, low_hits(rows), (((1,), (1,)), ((), ())), preferred_element_type=F32
    )
    return out[:tiles] + out[tiles : 2 * tiles] + out[2 * tiles :]


def arrived_rows(refs):
    return [ref[h : h + 1, :] for ref in refs for h in range(ref.shape[0])]


def store_sent(refs, sent):
    per = refs[0].shape[0]
    for k, ref in enumerate(refs):
        ref[...] = sent[k * per : (k + 1) * per, :]


def lane_rows(vector):
    return jnp.concatenate([vector[t : t + 1, :] for t in range(vector.shape[0])], axis=1)


def tile_rows_of(row):
    return jnp.concatenate(
        [row[:, t * LANES : (t + 1) * LANES] for t in range(row.shape[1] // LANES)], axis=0
    )


def fill_hits(hits, rows, first, last):
    nodes = hits.shape[0]
    node = lax.broadcasted_iota(jnp.int32, (nodes, LANES), 0).astype(jnp.int16).reshape(nodes // 16, 16, LANES)
    one, zero = jnp.ones(node.shape, BF16), jnp.zeros(node.shape, BF16)
    for c in range(first, last):
        wide = jnp.broadcast_to(rows[c], (16, LANES)).astype(jnp.int16)
        at = (c - first) * LANES
        hits[:, at : at + LANES] = jnp.where(node == wide[None], one, zero).reshape(nodes, LANES)


def gather_first(
    where, index_in, counts_in, state_in, lat, hits, places, sent, index, counts, state, sems
):
    first, second, third = copies(((index_in, index), (counts_in, counts), (state_in, state)), sems)
    per = index.shape[2] // LANES
    first.wait()
    second.wait()
    for g in range(index.shape[1]):
        side = where[g]
        for h in range(per):
            span = slice(h * LANES, (h + 1) * LANES)
            row = index[0, 0:1, span]
            for k in range(1, index.shape[1]):
                row = jnp.where(side == k, index[0, k : k + 1, span], row)
            slot = lax.broadcasted_iota(jnp.int32, (1, LANES), 1) + h * LANES
            r = g * per + h
            places[r : r + 1, :] = jnp.where(slot < counts[0, side], row, -1)
    fill_hits(hits, slot_rows(places), 0, per)
    third.wait()
    lat[...] = state[...].T
    send_features(lat[...], hits, (sent,))


def gather_rest(places, lat, gains_in, bias_in, decode_in, hits, columns, s1, s2, s3, gains, bias, decode, sems):
    waits = copies(((gains_in, gains), (bias_in, bias), (decode_in, decode)), sems)
    rows = slot_rows(places)
    fill_hits(hits, rows, len(rows) // 4, len(rows))
    send_features(lat[...], hits, (s1, s2, s3))
    for copy in waits:
        copy.wait()
    lines = [gains[layer] for layer in range(LAYERS)] + [bias[...], decode[...]]
    lines.append(jnp.zeros((8 - 3 * LAYERS - 1, bias.shape[1]), F32))
    columns[...] = jnp.concatenate(lines, axis=0).T


def send_features(lat, hits, outs):
    width = outs[0].shape[1]
    for k, out in enumerate(outs):
        out[...] = jnp.dot(
            lat, hits[:, k * width : (k + 1) * width], preferred_element_type=F32
        ).astype(BF16)


def send_rest(lat, hits, s1, s2, s3):
    send_features(lat[...], hits, (s1, s2, s3))


def build(
    tile_counts, places, tiles, lat, w_self, columns, rows_in, columns_in, capacity_in,
    matrix, half, inverse_rowsum, diagonal, local, own,
    tile_rows, tile_columns, capacity, sems,
):
    waits = copies(((rows_in, tile_rows), (columns_in, tile_columns), (capacity_in, capacity)), sems)
    count = tiles.shape[2]
    node_tiles = matrix.shape[0] // count
    matrix[...] = jnp.zeros(matrix.shape, F32)
    for t in range(node_tiles):
        span = slice(t * count, (t + 1) * count)
        block = tiles[0, t]
        matrix[span, span] = block + block.T
    for copy in waits:
        copy.wait()

    known = tiles.shape[1]
    live = tile_counts[0]
    together = 4

    def add(step, carry):
        for k in range(together):
            t = node_tiles + step * together + k
            at = jnp.minimum(t, known - 1)
            r = pl.multiple_of(tile_rows[0, at] * count, count)
            c = pl.multiple_of(tile_columns[0, at] * count, count)
            block = jnp.where(t < live, tiles[0, at], 0.0)
            matrix[pl.ds(r, count), pl.ds(c, count)] += block
            matrix[pl.ds(c, count), pl.ds(r, count)] += block.T
        return carry

    lax.fori_loop(0, (live - node_tiles + together - 1) // together, add, 0)
    rows = slot_rows(places)
    faces = spread_sum([jnp.ones((1, LANES), F32)] * len(rows), rows, node_tiles)
    total = jnp.zeros((8, matrix.shape[1]), F32)
    for t in range(node_tiles):
        block = matrix[t * count : (t + 1) * count, :]
        half[t * count : (t + 1) * count, :] = block.astype(BF16)
        total = total + jnp.sum(block.reshape(count // 8, 8, matrix.shape[1]), axis=0)
    rowsum = tile_rows_of(jnp.sum(total, axis=0, keepdims=True)) + faces
    inverse_rowsum[...] = lane_rows(1.0 / rowsum)
    diagonal[...] = capacity[...] + rowsum
    local[...] = jnp.dot(lat[...], half[...], preferred_element_type=F32)
    own[...] = own_part(0, lat[...], w_self, columns)


def normed(value, gain):
    scale = lax.rsqrt(jnp.mean(value * value, axis=0, keepdims=True) + 1e-06)
    return (value * scale * gain).astype(BF16)


def project(weight, value):
    return lax.dot_general(weight, value, (((0,), (0,)), ((), ())), preferred_element_type=F32)


def own_part(layer, lat, w_self, columns):
    gain = columns[:, 2 * layer : 2 * layer + 1]
    bias = columns[:, 2 * LAYERS + layer : 2 * LAYERS + layer + 1]
    return project(w_self[layer], normed(lat.astype(F32), gain)) + bias


def local_features(layer, lat, half, w_self, w_out, columns, local, own, before, decoder):
    local[...] = jnp.dot(lat[...], half[...], preferred_element_type=F32)
    own[...] = own_part(layer, lat[...], w_self, columns)
    decode = columns[:, 3 * LAYERS : 3 * LAYERS + 1]
    before[...] = jnp.sum(lat[...].astype(F32) * decode, axis=0, keepdims=True)
    line = jnp.broadcast_to(decode, (decode.shape[0], LANES)).T[0:1, :]
    decoder[...] = jnp.sum(w_out[layer].astype(F32) * line, axis=1, keepdims=True)


def with_slots(local, came, hits):
    return local + lax.dot_general(came, hits, (((1,), (1,)), ((), ())), preferred_element_type=F32)


def activation(layer, arrived, local, own, inverse_rowsum, first_hits, hits, w_neighbour, columns):
    total = with_slots(local[...], arrived[0][...], first_hits[...])
    total = with_slots(total, jnp.concatenate([a[...] for a in arrived[1:]], axis=1), hits[...])
    mean = total * inverse_rowsum[...]
    gain = columns[:, 2 * layer + 1 : 2 * layer + 2]
    linear = own[...] + project(w_neighbour[layer], normed(mean, gain))
    return linear / (1.0 + jnp.exp(-linear))


def first_layer(
    a0, a1, a2, a3, local, own, inverse_rowsum, lat, first_hits, hits, w_neighbour, w_out, columns, new, sent
):
    activated = activation(
        0, (a0, a1, a2, a3), local, own, inverse_rowsum, first_hits, hits, w_neighbour, columns
    ).astype(BF16)
    value = (lat[...].astype(F32) + project(w_out[0], activated)).astype(BF16)
    new[...] = value
    send_features(value, first_hits, (sent,))


def last_layer(
    places, a0, a1, a2, a3, local, own, inverse_rowsum, lat, first_hits, hits, w_neighbour, columns, before, decoder,
    guess, s0, s1, s2, s3,
):
    activated = activation(
        LAYERS - 1, (a0, a1, a2, a3), local, own, inverse_rowsum, first_hits, hits, w_neighbour, columns
    ).astype(BF16)
    row = before[...] + jnp.sum(activated.astype(F32) * decoder[...], axis=0, keepdims=True)
    field = tile_rows_of(row)
    guess[...] = field
    store_sent((s0, s1, s2, s3), pick(field, slot_rows(places)))


def product(matrix, field):
    count = LANES
    width = matrix.shape[1]
    total = jnp.zeros((8, width), F32)
    for t in range(field.shape[0]):
        column = jnp.broadcast_to(field[t : t + 1, :], (count, count)).T
        wide = jnp.concatenate([column] * (width // count), axis=1)
        part = matrix[t * count : (t + 1) * count, :] * wide
        total = total + jnp.sum(part.reshape(count // 8, 8, width), axis=0)
    return tile_rows_of(jnp.sum(total, axis=0, keepdims=True))


def matvec(matrix, vector, out):
    out[...] = product(matrix, vector[...])


def start_basis(places, a0, a1, a2, a3, local, guess, source, diagonal, basis, s0, s1, s2, s3):
    rows = slot_rows(places)
    came = spread_sum(arrived_rows((a0, a1, a2, a3)), rows, guess.shape[0])
    value = (source[...] + local[...] + came) / diagonal[...] - guess[...]
    basis[...] = value
    store_sent((s0, s1, s2, s3), pick(value, rows))


def next_basis(places, a0, a1, a2, a3, local, diagonal, basis, s0, s1, s2, s3):
    rows = slot_rows(places)
    came = spread_sum(arrived_rows((a0, a1, a2, a3)), rows, local.shape[0])
    value = (local[...] + came) / diagonal[...]
    basis[...] = value
    store_sent((s0, s1, s2, s3), pick(value, rows))


def diagonal_mask():
    return lax.broadcasted_iota(jnp.int32, (8, LANES), 0) == lax.broadcasted_iota(jnp.int32, (8, LANES), 1)


def last_basis(places, a0, a1, a2, a3, local, diagonal, b0, b1, matrix, basis, image, packets):
    rows = slot_rows(places)
    came = spread_sum(arrived_rows((a0, a1, a2, a3)), rows, local.shape[0])
    value = (local[...] + came) / diagonal[...]
    basis[...] = value
    mapped = product(matrix, value)
    image[...] = mapped
    held = [b0[...], b1[...], value]
    parts = []
    for k in range(2 * ITERS - 1):
        left, right = held[k // 2], held[(k + 1) // 2]
        parts.append(jnp.sum(left * right * diagonal[...], axis=0, keepdims=True))
    parts.append(jnp.sum(value * mapped, axis=0, keepdims=True))
    parts.append(jnp.zeros((8 - 2 * ITERS, LANES), F32))
    sums = jnp.sum(jnp.concatenate(parts, axis=0), axis=1, keepdims=True)
    row = jnp.sum(jnp.where(diagonal_mask(), sums, 0.0), axis=0, keepdims=True)
    packet = jnp.concatenate([lane_rows(pick(value, rows)), row], axis=1)
    for device in range(packets.shape[0]):
        packets[device] = packet


def added(values):
    values = list(values)
    while len(values) > 1:
        values = [sum(values[i : i + 2][1:], values[i]) for i in range(0, len(values), 2)]
    return values[0]


def finish(sizes, where, packets, places, image, guess, diagonal, b0, b1, b2, field, defect):
    doms, subs = sizes
    width = packets.shape[2] - LANES
    per = width // 4

    def slots(device, g):
        return packets[device, :, g * per : (g + 1) * per]

    edges = []
    for d in range(doms):
        for s in range(subs):
            for m, (i, j) in (((0, d % 2), (d + 1, s)), ((1, s % 2), (d, s + 1))):
                g = MATCHINGS.index(m)
                if i < doms and j < subs:
                    edges.append(slots(d * subs + s, g) * slots(i * subs + j, g))
    edges = added(edges)
    edges = added([edges[:, h : h + LANES] for h in range(0, per, LANES)])
    sums = added([packets[e, :, width : width + LANES] for e in range(doms * subs)])
    last_row = lax.broadcasted_iota(jnp.int32, (8, LANES), 0) == 2 * ITERS - 1
    table = jnp.where(diagonal_mask(), jnp.broadcast_to(sums, (8, LANES)), 0.0)
    table = table + jnp.where(last_row, jnp.broadcast_to(2.0 * edges, (8, LANES)), 0.0)
    columns = jnp.sum(table, axis=1, keepdims=True)
    n = [jnp.broadcast_to(columns[k : k + 1, :], (8, LANES)) for k in range(2 * ITERS)]
    came = []
    for g in range(4):
        mine = slots(where[4 + g], g)
        came += [mine[:, h : h + LANES] for h in range(0, per, LANES)]
    last = (image[...] + spread_sum(came, slot_rows(places), image.shape[0])) / diagonal[...]
    one, zero = jnp.ones((8, LANES), F32), jnp.zeros((8, LANES), F32)

    def paired(left, values):
        total = zero
        for i, a in enumerate(left):
            for j, b in enumerate(left):
                total = total + a * b * values[i + j]
        return total

    gaps = [n[k] - n[k + 1] for k in range(2 * ITERS - 1)]
    residual = [one]
    heading = [one]
    moved = [zero] * ITERS
    size = n[0]
    for step in range(ITERS):
        alpha = size / paired(heading, gaps)
        for i, h in enumerate(heading):
            moved[i] = moved[i] + alpha * h
        change = [
            (heading[i] if i < len(heading) else zero) - (heading[i - 1] if i > 0 else zero)
            for i in range(len(heading) + 1)
        ]
        residual = [
            (residual[i] if i < len(residual) else zero) - alpha * change[i]
            for i in range(len(change))
        ]
        if step + 1 < ITERS:
            following = paired(residual, n)
            beta = following / size
            heading = [
                residual[i] + (beta * heading[i] if i < len(heading) else zero)
                for i in range(len(residual))
            ]
            size = following
    held = [b0[...], b1[...], b2[...], last]
    total = guess[...]
    for c, b in zip(moved, held):
        total = total + c * b
    field[...] = total
    left = zero
    for c, b in zip(residual, held):
        left = left + c * b
    defect[...] = left * diagonal[...]


def mate_of(place, first, size):
    mate = ((place - first) ^ 1) + first
    return mate if place >= first and mate < size else None


def swaps(sizes, turn):
    along, first = MATCHINGS[turn]
    pairs = []
    for dom in range(sizes[0]):
        for sub in range(sizes[1]):
            to = [dom, sub]
            mate = mate_of(to[along], first, sizes[along])
            if mate is not None:
                to[along] = mate
            elif along == 1 and sizes[0] % 2 == 0:
                to[0] ^= 1
            elif along == 0 and sizes[1] % 2 == 0:
                to[1] = (sub + sizes[1] // 2) % sizes[1]
            pairs.append((dom * sizes[1] + sub, to[0] * sizes[1] + to[1]))
    return pairs


def places_of_turns():
    at = [lax.axis_index("dom"), lax.axis_index("sub")]
    sizes = [lax.axis_size("dom"), lax.axis_size("sub")]

    def side(along, first):
        odd = at[along] % 2
        return 2 * along + (odd if first else 1 - odd)

    def partner(along, first):
        mate = jnp.bitwise_xor(at[along] - first, 1) + first
        to = list(at)
        to[along] = jnp.where((at[along] >= first) & (mate < sizes[along]), mate, at[along])
        return to[0] * sizes[1] + to[1]

    out = [value(*m) for value in (side, partner) for m in MATCHINGS]
    return jnp.stack(out).astype(jnp.int32)


def swap(sent, turn):
    axes = ("dom", "sub")
    return lax.ppermute(sent, axes, swaps([lax.axis_size(axis) for axis in axes], turn))


def exchange(sent, first=0):
    return [swap(s, first + i) for i, s in enumerate(sent)]


def all_to_all(messages):
    return lax.all_to_all(messages, ("dom", "sub"), split_axis=0, concat_axis=0, tiled=True)


def per_device(
    state, tile_values, tile_rows, tile_columns, tile_counts, send_nodes, face_counts, capacity,
    source, w_self, w_neighbour, w_out, gains, bias, w_decode,
):
    nodes, width = state.shape
    slots = send_nodes.shape[2]
    tiles = nodes // LANES
    sizes = (lax.axis_size("dom"), lax.axis_size("sub"))
    devices = sizes[0] * sizes[1]
    field = shape((tiles, LANES))
    features = shape((width, nodes))
    vector_sent = [shape((slots // LANES, LANES))] * 4
    decode = w_decode.reshape(1, width)
    where = places_of_turns()
    capacity = capacity.reshape(tiles, LANES)
    source = source.reshape(tiles, LANES)

    one_sent = [shape((width, slots), BF16)]
    gather_flops = 2 * nodes * slots * width
    lat, first_hits, places, sent = run(
        gather_first,
        [shape((width, nodes), BF16), shape((nodes, slots), BF16), shape((4 * slots // LANES, LANES), jnp.int32)]
        + one_sent,
        (), (where,), (send_nodes, face_counts, state),
        (
            pltpu.VMEM(send_nodes.shape, jnp.int32),
            pltpu.SMEM(face_counts.shape, jnp.int32),
            pltpu.VMEM(state.shape, BF16),
        ),
        waits=3, flops=gather_flops,
    )
    a0 = swap(sent, 0)
    hits, columns, *sent = run(
        gather_rest, [shape((nodes, 3 * slots), BF16), shape((width, 8))] + one_sent * 3,
        (places, lat), (), (gains, bias, decode),
        (pltpu.VMEM(gains.shape, F32), pltpu.VMEM(bias.shape, F32), pltpu.VMEM(decode.shape, F32)),
        waits=3, flops=3 * gather_flops,
    )
    a1, a2, a3 = exchange(sent, 1)
    matrix, half, inverse_rowsum, diagonal, local, own = run(
        build,
        [shape((nodes, nodes)), shape((nodes, nodes), BF16), shape((1, nodes)), field, features, features],
        (places, tile_values, lat, w_self, columns),
        (tile_counts,), (tile_rows, tile_columns, capacity),
        (
            pltpu.SMEM(tile_rows.shape, jnp.int32),
            pltpu.SMEM(tile_columns.shape, jnp.int32),
            pltpu.VMEM(capacity.shape, F32),
        ),
        waits=3, flops=0, moved=0,
    )
    lat, sent = run(
        first_layer, [shape((width, nodes), BF16)] + one_sent,
        (a0, a1, a2, a3, local, own, inverse_rowsum, lat, first_hits, hits, w_neighbour, w_out, columns),
        flops=3 * nodes * nodes * width,
    )
    a0 = swap(sent, 0)
    sent = run(send_rest, one_sent * 3, (lat, hits), flops=3 * gather_flops)
    a1, a2, a3 = exchange(sent, 1)
    local, own, before, decoder = run(
        functools.partial(local_features, LAYERS - 1),
        [features, features, shape((1, nodes)), shape((width, 1))],
        (lat, half, w_self, w_out, columns), flops=0, moved=0,
    )
    guess, *sent = run(
        last_layer, [field] + vector_sent,
        (places, a0, a1, a2, a3, local, own, inverse_rowsum, lat, first_hits, hits, w_neighbour, columns, before, decoder),
        flops=3 * nodes * nodes * width,
    )

    def mapped(vector):
        return run(matvec, [field], (matrix, vector), flops=2 * nodes * nodes, moved=4 * nodes * nodes)[0]

    arrived = exchange(sent)
    local = mapped(guess)
    b0, *sent = run(
        start_basis, [field] + vector_sent, (places, *arrived, local, guess, source, diagonal)
    )
    arrived = exchange(sent)
    local = mapped(b0)
    b1, *sent = run(next_basis, [field] + vector_sent, (places, *arrived, local, diagonal))
    arrived = exchange(sent)
    local = mapped(b1)
    b2, image, packets = run(
        last_basis, [field, field, shape((devices, 1, 4 * slots + LANES))],
        (places, *arrived, local, diagonal, b0, b1, matrix),
    )
    packets = all_to_all(packets)
    heat, defect = run(
        functools.partial(finish, sizes), [field, field],
        (packets, places, image, guess, diagonal, b0, b1, b2), (where,),
    )
    return heat.reshape(nodes), defect.reshape(nodes)


def solution(mesh):
    both = ("dom", "sub")
    return jax.shard_map(
        per_device,
        mesh=mesh,
        in_specs=(
            P(both, None),
            P(both, None, None, None),
            P(both, None),
            P(both, None),
            P(both),
            P(both, None, None),
            P(both, None),
            P(both),
            P(both),
            P(),
            P(),
            P(),
            P(),
            P(),
            P(),
        ),
        out_specs=(P(both), P(both)),
        check_vma=False,
    )
```

profile of v0, /device:TPU:0, one launch (start us, length us, event | category | flops | bytes accessed | tf_op | source)
XLA Modules:
  0.0 55.9 jit_solution(17249416218501657634)
XLA Ops:
  0.8 2.0 %shard_map.158 = (bf16[256,1024]{1,0:T(8,128)(2,1)S(1)}, bf16[1024,256]{1,0:T(8,128)(2,1)S(1)}, s32[8,128]{1,0:T(8,128)S(1)}, bf16[256,256]{1,0:T(8,128)(2,1)S(1)}) custom-call(s32[8]{0:T(128)S(1)} %stack.35.where, s32[1,4,256]{2,1,0:T(4,128)} %index_in.1, s32[1,4]{1,0:T(1,128)} %counts_in.1, bf16[1024,256]{1,0:T(8,128)(2,1)} %state_in.1), custom_call_target="tpu_custom_call" | custom-call | flops 134217728 | bytes 1000000 | tf_op jit(solution)/shard_map/pallas_call | solution.py:29
  2.8 0.5 collective-permute-start
  3.3 1.3 %shard_map.159 = (bf16[1024,768]{1,0:T(8,128)(2,1)S(1)}, f32[256,8]{1,0:T(8,128)S(1)}, bf16[256,256]{1,0:T(8,128)(2,1)S(1)}, bf16[256,256]{1,0:T(8,128)(2,1)S(1)}, bf16[256,256]{1,0:T(8,128)(2,1)S(1)}) custom-call(s32[8,128]{1,0:T(8,128)S(1)} %get-tuple-element.46.places, bf16[256,1024]{1,0:T(8,128)(2,1)S(1)} %get-tuple-element.48.lat, ...), custom_call_target="tpu_custom_call" | custom-call | flops 402653184 | bytes 1000000 | tf_op jit(solution)/shard_map/pallas_call | solution.py:29
  4.6 4.0 %collective-permute-start.1 = (bf16[256,256]{1,0:T(8,128)(2,1)S(1)}, bf16[256,256]{1,0:T(8,128)(2,1)S(1)}, u32[]{:S(2)}, u32[]{:S(2)}) collective-permute-start(bf16[256,256]{1,0:T(8,128)(2,1)S(1)} %get-tuple-element.49), channel_id=1, source_target_pairs={{0,1},{1,0},{2,3},{3,2},{4,5},{5,4},{6,7},{7,6},{8,9},{9,8},{10,11... | collective-permute-start | bytes 393224 | tf_op jit(solution)/shard_map/ppermute | solution.py:454
  9.6 2.2 %shard_map.160 = (f32[1024,1024]{1,0:T(8,128)S(1)}, bf16[1024,1024]{1,0:T(8,128)(2,1)S(1)}, f32[1,1024]{1,0:T(1,128)S(1)}, f32[8,128]{1,0:T(8,128)S(1)}, f32[256...) custom-call(s32[1]{0:T(128)S(6)} %copy.17.tile_counts, s32[8,128]{1,0:T(8,128)S(1)} %get-tuple-element.46.places, ...), custom_call_target="tpu_custom_call" | custom-call | tf_op jit(solution)/shard_map/pallas_call | solution.py:29
  11.8 1.5 %collective-permute-done.1.a1 = bf16[256,256]{1,0:T(8,128)(2,1)S(1)} collective-permute-done((bf16[256,256]{1,0:T(8,128)(2,1)S(1)}, bf16[256,256]{1,0:T(8,128)(2,1)S(1)}, u32[]{:S(2)}, u32[]{:S(2)}) %collective-permute-start.1) | collective-permute-done | bytes 131104 | tf_op jit(solution)/shard_map/ppermute | solution.py:454
  13.3 0.3 collective-permute-done.3.a3
  13.6 1.6 %shard_map.161 = (bf16[256,1024]{1,0:T(8,128)(2,1)S(1)}, bf16[256,256]{1,0:T(8,128)(2,1)S(1)}) custom-call(bf16[256,256]{1,0:T(8,128)(2,1)S(1)} %collective-permute-done.a0, bf16[256,256]{1,0:T(8,128)(2,1)S(1)} %collective-permute-done.1.a1, bf16[256,256]{1,0:T(8,128)(2,1)S(1)} %collective-permute-done.2.a2, bf16[256,256]{1,0:T(8,128)(2,1)S(1)} %collective-permute-done.3.a3, ...), custom_call_target="tpu_custom_call" | custom-call | flops 805306368 | bytes 1000000 | tf_op jit(solution)/shard_map/pallas_call | solution.py:29
  15.5 0.6 %shard_map.162 = (bf16[256,256]{1,0:T(8,128)(2,1)S(1)}, bf16[256,256]{1,0:T(8,128)(2,1)S(1)}, bf16[256,256]{1,0:T(8,128)(2,1)S(1)}) custom-call(bf16[256,1024]{1,0:T(8,128)(2,1)S(1)} %get-tuple-element.59.lat, bf16[1024,768]{1,0:T(8,128)(2,1)S(1)} %get-tuple-element.57.hits), custom_call_target="tpu_custom_call" | custom-call | flops 402653184 | bytes 1000000 | tf_op jit(solution)/shard_map/pallas_call | solution.py:29
  16.1 1.9 %collective-permute-start.5 = (bf16[256,256]{1,0:T(8,128)(2,1)S(1)}, bf16[256,256]{1,0:T(8,128)(2,1)S(1)}, u32[]{:S(2)}, u32[]{:S(2)}) collective-permute-start(bf16[256,256]{1,0:T(8,128)(2,1)S(1)} %get-tuple-element.60), channel_id=1, source_target_pairs={{0,1},{1,0},{2,3},{3,2},{4,5},{5,4},{6,7},{7,6},{8,9},{9,8},{10,11... | collective-permute-start | bytes 393224 | tf_op jit(solution)/shard_map/ppermute | solution.py:454
  18.2 1.0 %shard_map.163 = (f32[256,1024]{1,0:T(8,128)S(1)}, f32[256,1024]{1,0:T(8,128)S(1)}, f32[1,1024]{1,0:T(1,128)S(1)}, f32[256,1]{1,0:T(8,128)S(1)}) custom-call(bf16[256,1024]{1,0:T(8,128)(2,1)S(1)} %get-tuple-element.59.lat, bf16[1024,1024]{1,0:T(8,128)(2,1)S(1)} %get-tuple-element.63.half, bf16[2,256,256]{2,1,0:T(8,128)(2,1)S(1)} %copy-done.1, ...), custom_call_target="tpu_custom_call" | custom-call | tf_op jit(solution)/shard_map/pallas_call | solution.py:29
  19.2 4.2 %collective-permute-done.5.a1 = bf16[256,256]{1,0:T(8,128)(2,1)S(1)} collective-permute-done((bf16[256,256]{1,0:T(8,128)(2,1)S(1)}, bf16[256,256]{1,0:T(8,128)(2,1)S(1)}, u32[]{:S(2)}, u32[]{:S(2)}) %collective-permute-start.5) | collective-permute-done | bytes 131104 | tf_op jit(solution)/shard_map/ppermute | solution.py:454
  23.5 1.4 %shard_map.164 = (f32[8,128]{1,0:T(8,128)S(1)}, f32[2,128]{1,0:T(2,128)S(1)}, f32[2,128]{1,0:T(2,128)S(1)}, f32[2,128]{1,0:T(2,128)S(1)}, f32[2,128]{1,0:T(2,128)S(1)}) custom-call(s32[8,128]{1,0:T(8,128)S(1)} %get-tuple-element.46.places, bf16[256,256]{1,0:T(8,128)(2,1)S(1)} %collective-permute-done.4.a0, bf16[256,256]{1,0:T(8,128)(2,1)S(1)} %collective-permute-done.5.a1, ...), custom_call_target="tpu_custom_call" | custom-call | flops 805306368 | bytes 1000000 | tf_op jit(solution)/shard_map/pallas_call | solution.py:29
  24.9 1.9 %collective-permute-start.9 = (f32[2,128]{1,0:T(2,128)S(1)}, f32[2,128]{1,0:T(2,128)S(1)}, u32[]{:S(2)}, u32[]{:S(2)}) collective-permute-start(f32[2,128]{1,0:T(2,128)S(1)} %get-tuple-element.69), channel_id=1, source_target_pairs={{0,1},{1,0},{2,3},{3,2},{4,5},{5,4},{6,7},{7,6},{8,9},{9,8},{10,11... | collective-permute-start | bytes 3080 | tf_op jit(solution)/shard_map/ppermute | solution.py:454
  27.0 0.3 shard_map.165.local
  27.3 1.2 %collective-permute-done.9.a1 = f32[2,128]{1,0:T(2,128)S(1)} collective-permute-done((f32[2,128]{1,0:T(2,128)S(1)}, f32[2,128]{1,0:T(2,128)S(1)}, u32[]{:S(2)}, u32[]{:S(2)}) %collective-permute-start.9) | collective-permute-done | bytes 1056 | tf_op jit(solution)/shard_map/ppermute | solution.py:454
  28.5 1.8 %collective-permute-done.11.a3 = f32[2,128]{1,0:T(2,128)S(1)} collective-permute-done((f32[2,128]{1,0:T(2,128)S(1)}, f32[2,128]{1,0:T(2,128)S(1)}, u32[]{:S(2)}, u32[]{:S(2)}) %collective-permute-start.11) | collective-permute-done | bytes 1056 | tf_op jit(solution)/shard_map/ppermute | solution.py:454
  30.3 0.3 shard_map.166
  30.7 1.6 %collective-permute-start.13 = (f32[2,128]{1,0:T(2,128)S(1)}, f32[2,128]{1,0:T(2,128)S(1)}, u32[]{:S(2)}, u32[]{:S(2)}) collective-permute-start(f32[2,128]{1,0:T(2,128)S(1)} %get-tuple-element.76), channel_id=1, source_target_pairs={{0,1},{1,0},{2,3},{3,2},{4,5},{5,4},{6,7},{7,6},{8,9},{9,8},{10,11... | collective-permute-start | bytes 3080 | tf_op jit(solution)/shard_map/ppermute | solution.py:454
  32.3 0.4 collective-permute-start.15
  32.7 0.3 shard_map.167.local
  33.1 1.2 %collective-permute-done.13.a1 = f32[2,128]{1,0:T(2,128)S(1)} collective-permute-done((f32[2,128]{1,0:T(2,128)S(1)}, f32[2,128]{1,0:T(2,128)S(1)}, u32[]{:S(2)}, u32[]{:S(2)}) %collective-permute-start.13) | collective-permute-done | bytes 1056 | tf_op jit(solution)/shard_map/ppermute | solution.py:454
  34.3 1.6 %collective-permute-done.15.a3 = f32[2,128]{1,0:T(2,128)S(1)} collective-permute-done((f32[2,128]{1,0:T(2,128)S(1)}, f32[2,128]{1,0:T(2,128)S(1)}, u32[]{:S(2)}, u32[]{:S(2)}) %collective-permute-start.15) | collective-permute-done | bytes 1056 | tf_op jit(solution)/shard_map/ppermute | solution.py:454
  35.9 0.3 shard_map.168
  36.3 1.8 %collective-permute-start.17 = (f32[2,128]{1,0:T(2,128)S(1)}, f32[2,128]{1,0:T(2,128)S(1)}, u32[]{:S(2)}, u32[]{:S(2)}) collective-permute-start(f32[2,128]{1,0:T(2,128)S(1)} %get-tuple-element.81), channel_id=1, source_target_pairs={{0,1},{1,0},{2,3},{3,2},{4,5},{5,4},{6,7},{7,6},{8,9},{9,8},{10,11... | collective-permute-start | bytes 3080 | tf_op jit(solution)/shard_map/ppermute | solution.py:454
  38.1 0.5 collective-permute-start.19
  38.6 0.3 shard_map.169.local
  39.0 0.9 %collective-permute-done.17.a1 = f32[2,128]{1,0:T(2,128)S(1)} collective-permute-done((f32[2,128]{1,0:T(2,128)S(1)}, f32[2,128]{1,0:T(2,128)S(1)}, u32[]{:S(2)}, u32[]{:S(2)}) %collective-permute-start.17) | collective-permute-done | bytes 1056 | tf_op jit(solution)/shard_map/ppermute | solution.py:454
  39.9 1.8 %collective-permute-done.19.a3 = f32[2,128]{1,0:T(2,128)S(1)} collective-permute-done((f32[2,128]{1,0:T(2,128)S(1)}, f32[2,128]{1,0:T(2,128)S(1)}, u32[]{:S(2)}, u32[]{:S(2)}) %collective-permute-start.19) | collective-permute-done | bytes 1056 | tf_op jit(solution)/shard_map/ppermute | solution.py:454
  41.7 0.7 %shard_map.170 = (f32[8,128]{1,0:T(8,128)S(1)}, f32[8,128]{1,0:T(8,128)S(1)}, f32[32,1,1152]{2,1,0:T(1,128)S(1)}) custom-call(s32[8,128]{1,0:T(8,128)S(1)} %get-tuple-element.46.places, f32[2,128]{1,0:T(2,128)S(1)} %collective-permute-done.16.a0, f32[2,128]{1,0:T(2,128)S(1)} %collective-permute-done.17.a1, f32[2,128]{1,0:T(2,128)S(1)} %collective-permute-done.18.a2, ...), custom_call_target="tpu_custom_call" | custom-call | flops 1000000 | bytes 1000000 | tf_op jit(solution)/shard_map/pallas_call | solution.py:29
  42.4 12.2 %all_to_all.5.packets = f32[32,1,1152]{2,1,0:T(1,128)S(1)} all-to-all(f32[32,1,1152]{2,1,0:T(1,128)S(1)} %get-tuple-element.85), channel_id=1, replica_groups=mesh['dom'=8,'sub'=4] {'dom','sub'}, dimensions={0} | all-to-all | bytes 294912 | tf_op jit(solution)/shard_map/all_to_all | solution.py:462
  54.5 1.4 %shard_map.171 = (f32[8,128]{1,0:T(8,128)}, f32[8,128]{1,0:T(8,128)}) custom-call(s32[8]{0:T(128)S(1)} %stack.35.where, f32[32,1,1152]{2,1,0:T(1,128)S(1)} %all_to_all.5.packets, s32[8,128]{1,0:T(8,128)S(1)} %get-tuple-element.46.places, f32[8,128]{1,0:T(8,128)S(1)} %get-tuple-element.86.image, f32[8,128]{1,0:T(8,128)S(1)} %get-tuple-element.73.vector.guess, ...), custom_call_target="tpu_custom_call" | custom-call | flops 1000000 | bytes 1000000 | tf_op jit(solution)/shard_map/pallas_call | solution.py:29
  (34 shorter events, 1.4 us)
Async XLA Ops:
  0.6 8.9 %copy-start.1 = (bf16[2,256,256]{2,1,0:T(8,128)(2,1)S(1)}, bf16[2,256,256]{2,1,0:T(8,128)(2,1)}, u32[]{:S(2)}) copy-start(bf16[2,256,256]{2,1,0:T(8,128)(2,1)} %w_self.3) | copy-start | bytes 786436
  0.6 8.9 %copy-start = (f32[1,24,128,128]{3,2,1,0:T(8,128)S(1)}, f32[1,24,128,128]{3,2,1,0:T(8,128)}, u32[]{:S(2)}) copy-start(f32[1,24,128,128]{3,2,1,0:T(8,128)} %tiles.1) | copy-start | bytes 4718596
  2.8 10.9 %copy-start.2 = (bf16[2,256,256]{2,1,0:T(8,128)(2,1)S(1)}, bf16[2,256,256]{2,1,0:T(8,128)(2,1)}, u32[]{:S(2)}) copy-start(bf16[2,256,256]{2,1,0:T(8,128)(2,1)} %w_out.3) | copy-start | bytes 786436
  2.8 10.9 %copy-start.3 = (bf16[2,256,256]{2,1,0:T(8,128)(2,1)S(1)}, bf16[2,256,256]{2,1,0:T(8,128)(2,1)}, u32[]{:S(2)}) copy-start(bf16[2,256,256]{2,1,0:T(8,128)(2,1)} %w_neighbour.3) | copy-start | bytes 786436
  2.8 9.0 %collective-permute-start = (bf16[256,256]{1,0:T(8,128)(2,1)S(1)}, bf16[256,256]{1,0:T(8,128)(2,1)S(1)}, u32[]{:S(2)}, u32[]{:S(2)}) collective-permute-start(bf16[256,256]{1,0:T(8,128)(2,1)S(1)} %get-tuple-element.47), channel_id=1, source_target_pairs={{0,4},{1,2},{2,1},{3,7},{4,0},{5,6},{6,5},{7,3},{8,12},{9,10},{10,... | collective-permute-start | bytes 393224 | tf_op jit(solution)/shard_map/ppermute | solution.py:454
  4.6 8.7 %collective-permute-start.1 = (bf16[256,256]{1,0:T(8,128)(2,1)S(1)}, bf16[256,256]{1,0:T(8,128)(2,1)S(1)}, u32[]{:S(2)}, u32[]{:S(2)}) collective-permute-start(bf16[256,256]{1,0:T(8,128)(2,1)S(1)} %get-tuple-element.49), channel_id=1, source_target_pairs={{0,1},{1,0},{2,3},{3,2},{4,5},{5,4},{6,7},{7,6},{8,9},{9,8},{10,11... | collective-permute-start | bytes 393224 | tf_op jit(solution)/shard_map/ppermute | solution.py:454
  8.7 4.6 %collective-permute-start.2 = (bf16[256,256]{1,0:T(8,128)(2,1)S(1)}, bf16[256,256]{1,0:T(8,128)(2,1)S(1)}, u32[]{:S(2)}, u32[]{:S(2)}) collective-permute-start(bf16[256,256]{1,0:T(8,128)(2,1)S(1)} %get-tuple-element.50), channel_id=1, source_target_pairs={{0,4},{1,5},{2,6},{3,7},{4,0},{5,1},{6,2},{7,3},{8,12},{9,13},{10,... | collective-permute-start | bytes 393224 | tf_op jit(solution)/shard_map/ppermute | solution.py:454
  8.7 5.0 %collective-permute-start.3 = (bf16[256,256]{1,0:T(8,128)(2,1)S(1)}, bf16[256,256]{1,0:T(8,128)(2,1)S(1)}, u32[]{:S(2)}, u32[]{:S(2)}) collective-permute-start(bf16[256,256]{1,0:T(8,128)(2,1)S(1)} %get-tuple-element.51), channel_id=1, source_target_pairs={{0,2},{1,3},{2,0},{3,1},{4,8},{5,9},{6,10},{7,11},{8,4},{9,5},{10,... | collective-permute-start | bytes 393224 | tf_op jit(solution)/shard_map/ppermute | solution.py:454
  15.3 4.0 %collective-permute-start.4 = (bf16[256,256]{1,0:T(8,128)(2,1)S(1)}, bf16[256,256]{1,0:T(8,128)(2,1)S(1)}, u32[]{:S(2)}, u32[]{:S(2)}) collective-permute-start(bf16[256,256]{1,0:T(8,128)(2,1)S(1)} %get-tuple-element.58), channel_id=1, source_target_pairs={{0,4},{1,2},{2,1},{3,7},{4,0},{5,6},{6,5},{7,3},{8,12},{9,10},{10,... | collective-permute-start | bytes 393224 | tf_op jit(solution)/shard_map/ppermute | solution.py:454
  16.1 7.3 %collective-permute-start.5 = (bf16[256,256]{1,0:T(8,128)(2,1)S(1)}, bf16[256,256]{1,0:T(8,128)(2,1)S(1)}, u32[]{:S(2)}, u32[]{:S(2)}) collective-permute-start(bf16[256,256]{1,0:T(8,128)(2,1)S(1)} %get-tuple-element.60), channel_id=1, source_target_pairs={{0,1},{1,0},{2,3},{3,2},{4,5},{5,4},{6,7},{7,6},{8,9},{9,8},{10,11... | collective-permute-start | bytes 393224 | tf_op jit(solution)/shard_map/ppermute | solution.py:454
  18.0 5.4 %collective-permute-start.6 = (bf16[256,256]{1,0:T(8,128)(2,1)S(1)}, bf16[256,256]{1,0:T(8,128)(2,1)S(1)}, u32[]{:S(2)}, u32[]{:S(2)}) collective-permute-start(bf16[256,256]{1,0:T(8,128)(2,1)S(1)} %get-tuple-element.61), channel_id=1, source_target_pairs={{0,4},{1,5},{2,6},{3,7},{4,0},{5,1},{6,2},{7,3},{8,12},{9,13},{10,... | collective-permute-start | bytes 393224 | tf_op jit(solution)/shard_map/ppermute | solution.py:454
  18.0 5.4 %collective-permute-start.7 = (bf16[256,256]{1,0:T(8,128)(2,1)S(1)}, bf16[256,256]{1,0:T(8,128)(2,1)S(1)}, u32[]{:S(2)}, u32[]{:S(2)}) collective-permute-start(bf16[256,256]{1,0:T(8,128)(2,1)S(1)} %get-tuple-element.62), channel_id=1, source_target_pairs={{0,2},{1,3},{2,0},{3,1},{4,8},{5,9},{6,10},{7,11},{8,4},{9,5},{10,... | collective-permute-start | bytes 393224 | tf_op jit(solution)/shard_map/ppermute | solution.py:454
  24.8 2.5 %collective-permute-start.8 = (f32[2,128]{1,0:T(2,128)S(1)}, f32[2,128]{1,0:T(2,128)S(1)}, u32[]{:S(2)}, u32[]{:S(2)}) collective-permute-start(f32[2,128]{1,0:T(2,128)S(1)} %get-tuple-element.68), channel_id=1, source_target_pairs={{0,4},{1,2},{2,1},{3,7},{4,0},{5,6},{6,5},{7,3},{8,12},{9,10},{10,... | collective-permute-start | bytes 3080 | tf_op jit(solution)/shard_map/ppermute | solution.py:454
  24.9 3.6 %collective-permute-start.9 = (f32[2,128]{1,0:T(2,128)S(1)}, f32[2,128]{1,0:T(2,128)S(1)}, u32[]{:S(2)}, u32[]{:S(2)}) collective-permute-start(f32[2,128]{1,0:T(2,128)S(1)} %get-tuple-element.69), channel_id=1, source_target_pairs={{0,1},{1,0},{2,3},{3,2},{4,5},{5,4},{6,7},{7,6},{8,9},{9,8},{10,11... | collective-permute-start | bytes 3080 | tf_op jit(solution)/shard_map/ppermute | solution.py:454
  26.7 1.8 %collective-permute-start.10 = (f32[2,128]{1,0:T(2,128)S(1)}, f32[2,128]{1,0:T(2,128)S(1)}, u32[]{:S(2)}, u32[]{:S(2)}) collective-permute-start(f32[2,128]{1,0:T(2,128)S(1)} %get-tuple-element.70), channel_id=1, source_target_pairs={{0,4},{1,5},{2,6},{3,7},{4,0},{5,1},{6,2},{7,3},{8,12},{9,13},{10,... | collective-permute-start | bytes 3080 | tf_op jit(solution)/shard_map/ppermute | solution.py:454
  26.7 3.6 %collective-permute-start.11 = (f32[2,128]{1,0:T(2,128)S(1)}, f32[2,128]{1,0:T(2,128)S(1)}, u32[]{:S(2)}, u32[]{:S(2)}) collective-permute-start(f32[2,128]{1,0:T(2,128)S(1)} %get-tuple-element.71), channel_id=1, source_target_pairs={{0,2},{1,3},{2,0},{3,1},{4,8},{5,9},{6,10},{7,11},{8,4},{9,5},{10,... | collective-permute-start | bytes 3080 | tf_op jit(solution)/shard_map/ppermute | solution.py:454
  27.0 3.4 %copy-start.4 = (f32[1024]{0:T(1024)S(1)}, f32[1024]{0:T(1024)}, u32[]{:S(2)}) copy-start(f32[1024]{0:T(1024)} %param.23) | copy-start | bytes 12292
  30.6 2.5 %collective-permute-start.12 = (f32[2,128]{1,0:T(2,128)S(1)}, f32[2,128]{1,0:T(2,128)S(1)}, u32[]{:S(2)}, u32[]{:S(2)}) collective-permute-start(f32[2,128]{1,0:T(2,128)S(1)} %get-tuple-element.75), channel_id=1, source_target_pairs={{0,4},{1,2},{2,1},{3,7},{4,0},{5,6},{6,5},{7,3},{8,12},{9,10},{10,... | collective-permute-start | bytes 3080 | tf_op jit(solution)/shard_map/ppermute | solution.py:454
  30.7 3.6 %collective-permute-start.13 = (f32[2,128]{1,0:T(2,128)S(1)}, f32[2,128]{1,0:T(2,128)S(1)}, u32[]{:S(2)}, u32[]{:S(2)}) collective-permute-start(f32[2,128]{1,0:T(2,128)S(1)} %get-tuple-element.76), channel_id=1, source_target_pairs={{0,1},{1,0},{2,3},{3,2},{4,5},{5,4},{6,7},{7,6},{8,9},{9,8},{10,11... | collective-permute-start | bytes 3080 | tf_op jit(solution)/shard_map/ppermute | solution.py:454
  32.3 2.0 %collective-permute-start.14 = (f32[2,128]{1,0:T(2,128)S(1)}, f32[2,128]{1,0:T(2,128)S(1)}, u32[]{:S(2)}, u32[]{:S(2)}) collective-permute-start(f32[2,128]{1,0:T(2,128)S(1)} %get-tuple-element.77), channel_id=1, source_target_pairs={{0,4},{1,5},{2,6},{3,7},{4,0},{5,1},{6,2},{7,3},{8,12},{9,13},{10,... | collective-permute-start | bytes 3080 | tf_op jit(solution)/shard_map/ppermute | solution.py:454
  32.3 3.6 %collective-permute-start.15 = (f32[2,128]{1,0:T(2,128)S(1)}, f32[2,128]{1,0:T(2,128)S(1)}, u32[]{:S(2)}, u32[]{:S(2)}) collective-permute-start(f32[2,128]{1,0:T(2,128)S(1)} %get-tuple-element.78), channel_id=1, source_target_pairs={{0,2},{1,3},{2,0},{3,1},{4,8},{5,9},{6,10},{7,11},{8,4},{9,5},{10,... | collective-permute-start | bytes 3080 | tf_op jit(solution)/shard_map/ppermute | solution.py:454
  36.2 2.8 %collective-permute-start.16 = (f32[2,128]{1,0:T(2,128)S(1)}, f32[2,128]{1,0:T(2,128)S(1)}, u32[]{:S(2)}, u32[]{:S(2)}) collective-permute-start(f32[2,128]{1,0:T(2,128)S(1)} %get-tuple-element.80), channel_id=1, source_target_pairs={{0,4},{1,2},{2,1},{3,7},{4,0},{5,6},{6,5},{7,3},{8,12},{9,10},{10,... | collective-permute-start | bytes 3080 | tf_op jit(solution)/shard_map/ppermute | solution.py:454
  36.3 3.6 %collective-permute-start.17 = (f32[2,128]{1,0:T(2,128)S(1)}, f32[2,128]{1,0:T(2,128)S(1)}, u32[]{:S(2)}, u32[]{:S(2)}) collective-permute-start(f32[2,128]{1,0:T(2,128)S(1)} %get-tuple-element.81), channel_id=1, source_target_pairs={{0,1},{1,0},{2,3},{3,2},{4,5},{5,4},{6,7},{7,6},{8,9},{9,8},{10,11... | collective-permute-start | bytes 3080 | tf_op jit(solution)/shard_map/ppermute | solution.py:454
  38.1 1.8 %collective-permute-start.18 = (f32[2,128]{1,0:T(2,128)S(1)}, f32[2,128]{1,0:T(2,128)S(1)}, u32[]{:S(2)}, u32[]{:S(2)}) collective-permute-start(f32[2,128]{1,0:T(2,128)S(1)} %get-tuple-element.82), channel_id=1, source_target_pairs={{0,4},{1,5},{2,6},{3,7},{4,0},{5,1},{6,2},{7,3},{8,12},{9,13},{10,... | collective-permute-start | bytes 3080 | tf_op jit(solution)/shard_map/ppermute | solution.py:454
  38.1 3.6 %collective-permute-start.19 = (f32[2,128]{1,0:T(2,128)S(1)}, f32[2,128]{1,0:T(2,128)S(1)}, u32[]{:S(2)}, u32[]{:S(2)}) collective-permute-start(f32[2,128]{1,0:T(2,128)S(1)} %get-tuple-element.83), channel_id=1, source_target_pairs={{0,2},{1,3},{2,0},{3,1},{4,8},{5,9},{6,10},{7,11},{8,4},{9,5},{10,... | collective-permute-start | bytes 3080 | tf_op jit(solution)/shard_map/ppermute | solution.py:454
where the time goes:
time: 55.9 us
  waiting for transfers between devices  14.5 us (26%)
  starting transfers between devices  13.9 us (25%)
  Pallas kernels  13.8 us (25%)
  blocking collectives  12.2 us (22%)
  between operations  1.53 us (3%)
    ppermute x20, waiting for transfers between devices, swap(): lax.ppermute(sent, axes, swaps([lax.axis_size(axis) for axis in axes], tu...  14.5 us
    ppermute x20, starting transfers between devices, swap(): lax.ppermute(sent, axes, swaps([lax.axis_size(axis) for axis in axes], tu...  13.9 us
    pallas_call x14, Pallas kernels, run(): pl.pallas_call(body, out_shape=outs, in_specs=[smem] * len(scalars) + [vm...  13.8 us
    all_to_all x1, blocking collectives, all_to_all(): lax.all_to_all(messages, ('dom', 'sub'), split_axis=0, concat_axis=0, til...  12.2 us
  transfers between devices with their start and end apart: 20, of which 9 were waited for; matrix products, arithmetic and copies ran while one was open for 0% of the time, Pallas kernels for 11%

commit v1 on v0

--- a/solution.py
+++ b/solution.py
@@ -414,7 +414,7 @@
     return mate if place >= first and mate < size else None
 
 
-def swaps(sizes, turn):
+def swaps(sizes, turn, mirrored):
     along, first = MATCHINGS[turn]
     pairs = []
     for dom in range(sizes[0]):
@@ -426,7 +426,7 @@
             elif along == 1 and sizes[0] % 2 == 0:
                 to[0] ^= 1
             elif along == 0 and sizes[1] % 2 == 0:
-                to[1] = (sub + sizes[1] // 2) % sizes[1]
+                to[1] = sizes[1] - 1 - sub if mirrored else (sub + sizes[1] // 2) % sizes[1]
             pairs.append((dom * sizes[1] + sub, to[0] * sizes[1] + to[1]))
     return pairs
 
@@ -451,7 +451,8 @@
 
 def swap(sent, turn):
     axes = ("dom", "sub")
-    return lax.ppermute(sent, axes, swaps([lax.axis_size(axis) for axis in axes], turn))
+    small = sent.dtype == F32
+    return lax.ppermute(sent, axes, swaps([lax.axis_size(axis) for axis in axes], turn, small))
 
 
 def exchange(sent, first=0):

time: 55.9 us -> 57.1 us (1.021)
  starting transfers between devices: 13.9 us -> 17.3 us
  blocking collectives: 12.2 us -> 10.4 us
  waiting for transfers between devices: 14.5 us -> 13.7 us
    ppermute x20, starting transfers between devices: 13.9 us -> 17.3 us  [swap(): lax.ppermute(sent, axes, swaps([lax.axis_size(axis) for axis in axes], tu...]
    all_to_all x1, blocking collectives: 12.2 us -> 10.4 us  [all_to_all(): lax.all_to_all(messages, ('dom', 'sub'), split_axis=0, concat_axis=0, til...]
    ppermute x20, waiting for transfers between devices: 14.5 us -> 13.7 us  [swap(): lax.ppermute(sent, axes, swaps([lax.axis_size(axis) for axis in axes], tu...]
  transfers between devices with their start and end apart: 20 -> 20, of which waited for: 9 -> 7; matrix products, arithmetic and copies ran while one was open for 0% -> 0% of each run, Pallas kernels for 11% -> 11%
where the time goes in v1:
time: 57.1 us; the launch traced here: 56.9 us
  starting transfers between devices  17.3 us (30%)
  Pallas kernels  13.8 us (24%)
  waiting for transfers between devices  13.7 us (24%)
  blocking collectives  10.4 us (18%)
  between operations  1.57 us (3%)
    ppermute x20, starting transfers between devices, swap(): lax.ppermute(sent, axes, swaps([lax.axis_size(axis) for axis in axes], tu...  17.3 us
    pallas_call x14, Pallas kernels, run(): pl.pallas_call(body, out_shape=outs, in_specs=[smem] * len(scalars) + [vm...  13.8 us
    ppermute x20, waiting for transfers between devices, swap(): lax.ppermute(sent, axes, swaps([lax.axis_size(axis) for axis in axes], tu...  13.7 us
    all_to_all x1, blocking collectives, all_to_all(): lax.all_to_all(messages, ('dom', 'sub'), split_axis=0, concat_axis=0, til...  10.4 us
  transfers between devices with their start and end apart: 20, of which 7 were waited for; matrix products, arithmetic and copies ran while one was open for 0% of the time, Pallas kernels for 11%

profile of v1, /device:TPU:0, one launch (start us, length us, event | category | flops | bytes accessed | tf_op | source)
XLA Modules:
  0.0 56.9 jit_solution(3786280821779157590)
XLA Ops:
  0.8 2.0 %shard_map.158 = (bf16[256,1024]{1,0:T(8,128)(2,1)S(1)}, bf16[1024,256]{1,0:T(8,128)(2,1)S(1)}, s32[8,128]{1,0:T(8,128)S(1)}, bf16[256,256]{1,0:T(8,128)(2,1)S(1)}) custom-call(s32[8]{0:T(128)S(1)} %stack.35.where, s32[1,4,256]{2,1,0:T(4,128)} %index_in.1, s32[1,4]{1,0:T(1,128)} %counts_in.1, bf16[1024,256]{1,0:T(8,128)(2,1)} %state_in.1), custom_call_target="tpu_custom_call" | custom-call | flops 134217728 | bytes 1000000 | tf_op jit(solution)/shard_map/pallas_call | solution.py:29
  2.8 0.5 collective-permute-start
  3.3 1.3 %shard_map.159 = (bf16[1024,768]{1,0:T(8,128)(2,1)S(1)}, f32[256,8]{1,0:T(8,128)S(1)}, bf16[256,256]{1,0:T(8,128)(2,1)S(1)}, bf16[256,256]{1,0:T(8,128)(2,1)S(1)}, bf16[256,256]{1,0:T(8,128)(2,1)S(1)}) custom-call(s32[8,128]{1,0:T(8,128)S(1)} %get-tuple-element.46.places, bf16[256,1024]{1,0:T(8,128)(2,1)S(1)} %get-tuple-element.48.lat, ...), custom_call_target="tpu_custom_call" | custom-call | flops 402653184 | bytes 1000000 | tf_op jit(solution)/shard_map/pallas_call | solution.py:29
  4.6 4.0 %collective-permute-start.1 = (bf16[256,256]{1,0:T(8,128)(2,1)S(1)}, bf16[256,256]{1,0:T(8,128)(2,1)S(1)}, u32[]{:S(2)}, u32[]{:S(2)}) collective-permute-start(bf16[256,256]{1,0:T(8,128)(2,1)S(1)} %get-tuple-element.49), channel_id=1, source_target_pairs={{0,1},{1,0},{2,3},{3,2},{4,5},{5,4},{6,7},{7,6},{8,9},{9,8},{10,11... | collective-permute-start | bytes 393224 | tf_op jit(solution)/shard_map/ppermute | solution.py:455
  8.7 0.3 collective-permute-start.3
  9.6 2.2 %shard_map.160 = (f32[1024,1024]{1,0:T(8,128)S(1)}, bf16[1024,1024]{1,0:T(8,128)(2,1)S(1)}, f32[1,1024]{1,0:T(1,128)S(1)}, f32[8,128]{1,0:T(8,128)S(1)}, f32[256...) custom-call(s32[1]{0:T(128)S(6)} %copy.17.tile_counts, s32[8,128]{1,0:T(8,128)S(1)} %get-tuple-element.46.places, ...), custom_call_target="tpu_custom_call" | custom-call | tf_op jit(solution)/shard_map/pallas_call | solution.py:29
  11.8 1.5 %collective-permute-done.1.a1 = bf16[256,256]{1,0:T(8,128)(2,1)S(1)} collective-permute-done((bf16[256,256]{1,0:T(8,128)(2,1)S(1)}, bf16[256,256]{1,0:T(8,128)(2,1)S(1)}, u32[]{:S(2)}, u32[]{:S(2)}) %collective-permute-start.1) | collective-permute-done | bytes 131104 | tf_op jit(solution)/shard_map/ppermute | solution.py:455
  13.3 0.3 collective-permute-done.3.a3
  13.6 1.6 %shard_map.161 = (bf16[256,1024]{1,0:T(8,128)(2,1)S(1)}, bf16[256,256]{1,0:T(8,128)(2,1)S(1)}) custom-call(bf16[256,256]{1,0:T(8,128)(2,1)S(1)} %collective-permute-done.a0, bf16[256,256]{1,0:T(8,128)(2,1)S(1)} %collective-permute-done.1.a1, bf16[256,256]{1,0:T(8,128)(2,1)S(1)} %collective-permute-done.2.a2, bf16[256,256]{1,0:T(8,128)(2,1)S(1)} %collective-permute-done.3.a3, ...), custom_call_target="tpu_custom_call" | custom-call | flops 805306368 | bytes 1000000 | tf_op jit(solution)/shard_map/pallas_call | solution.py:29
  15.4 0.6 %shard_map.162 = (bf16[256,256]{1,0:T(8,128)(2,1)S(1)}, bf16[256,256]{1,0:T(8,128)(2,1)S(1)}, bf16[256,256]{1,0:T(8,128)(2,1)S(1)}) custom-call(bf16[256,1024]{1,0:T(8,128)(2,1)S(1)} %get-tuple-element.59.lat, bf16[1024,768]{1,0:T(8,128)(2,1)S(1)} %get-tuple-element.57.hits), custom_call_target="tpu_custom_call" | custom-call | flops 402653184 | bytes 1000000 | tf_op jit(solution)/shard_map/pallas_call | solution.py:29
  16.0 2.0 %collective-permute-start.5 = (bf16[256,256]{1,0:T(8,128)(2,1)S(1)}, bf16[256,256]{1,0:T(8,128)(2,1)S(1)}, u32[]{:S(2)}, u32[]{:S(2)}) collective-permute-start(bf16[256,256]{1,0:T(8,128)(2,1)S(1)} %get-tuple-element.60), channel_id=1, source_target_pairs={{0,1},{1,0},{2,3},{3,2},{4,5},{5,4},{6,7},{7,6},{8,9},{9,8},{10,11... | collective-permute-start | bytes 393224 | tf_op jit(solution)/shard_map/ppermute | solution.py:455
  18.0 0.2 collective-permute-start.7
  18.2 1.0 %shard_map.163 = (f32[256,1024]{1,0:T(8,128)S(1)}, f32[256,1024]{1,0:T(8,128)S(1)}, f32[1,1024]{1,0:T(1,128)S(1)}, f32[256,1]{1,0:T(8,128)S(1)}) custom-call(bf16[256,1024]{1,0:T(8,128)(2,1)S(1)} %get-tuple-element.59.lat, bf16[1024,1024]{1,0:T(8,128)(2,1)S(1)} %get-tuple-element.63.half, bf16[2,256,256]{2,1,0:T(8,128)(2,1)S(1)} %copy-done.1, ...), custom_call_target="tpu_custom_call" | custom-call | tf_op jit(solution)/shard_map/pallas_call | solution.py:29
  19.2 4.0 %collective-permute-done.5.a1 = bf16[256,256]{1,0:T(8,128)(2,1)S(1)} collective-permute-done((bf16[256,256]{1,0:T(8,128)(2,1)S(1)}, bf16[256,256]{1,0:T(8,128)(2,1)S(1)}, u32[]{:S(2)}, u32[]{:S(2)}) %collective-permute-start.5) | collective-permute-done | bytes 131104 | tf_op jit(solution)/shard_map/ppermute | solution.py:455
  23.3 1.4 %shard_map.164 = (f32[8,128]{1,0:T(8,128)S(1)}, f32[2,128]{1,0:T(2,128)S(1)}, f32[2,128]{1,0:T(2,128)S(1)}, f32[2,128]{1,0:T(2,128)S(1)}, f32[2,128]{1,0:T(2,128)S(1)}) custom-call(s32[8,128]{1,0:T(8,128)S(1)} %get-tuple-element.46.places, bf16[256,256]{1,0:T(8,128)(2,1)S(1)} %collective-permute-done.4.a0, bf16[256,256]{1,0:T(8,128)(2,1)S(1)} %collective-permute-done.5.a1, ...), custom_call_target="tpu_custom_call" | custom-call | flops 805306368 | bytes 1000000 | tf_op jit(solution)/shard_map/pallas_call | solution.py:29
  24.7 2.1 %collective-permute-start.9 = (f32[2,128]{1,0:T(2,128)S(1)}, f32[2,128]{1,0:T(2,128)S(1)}, u32[]{:S(2)}, u32[]{:S(2)}) collective-permute-start(f32[2,128]{1,0:T(2,128)S(1)} %get-tuple-element.69), channel_id=1, source_target_pairs={{0,1},{1,0},{2,3},{3,2},{4,5},{5,4},{6,7},{7,6},{8,9},{9,8},{10,11... | collective-permute-start | bytes 3080 | tf_op jit(solution)/shard_map/ppermute | solution.py:455
  26.8 1.3 %collective-permute-start.11 = (f32[2,128]{1,0:T(2,128)S(1)}, f32[2,128]{1,0:T(2,128)S(1)}, u32[]{:S(2)}, u32[]{:S(2)}) collective-permute-start(f32[2,128]{1,0:T(2,128)S(1)} %get-tuple-element.71), channel_id=1, source_target_pairs={{0,3},{1,2},{2,1},{3,0},{4,8},{5,9},{6,10},{7,11},{8,4},{9,5},{10,... | collective-permute-start | bytes 3080 | tf_op jit(solution)/shard_map/ppermute | solution.py:455
  28.1 0.3 shard_map.165.local
  28.5 2.8 %collective-permute-done.11.a3 = f32[2,128]{1,0:T(2,128)S(1)} collective-permute-done((f32[2,128]{1,0:T(2,128)S(1)}, f32[2,128]{1,0:T(2,128)S(1)}, u32[]{:S(2)}, u32[]{:S(2)}) %collective-permute-start.11) | collective-permute-done | bytes 1056 | tf_op jit(solution)/shard_map/ppermute | solution.py:455
  31.2 0.3 shard_map.166
  31.6 1.6 %collective-permute-start.13 = (f32[2,128]{1,0:T(2,128)S(1)}, f32[2,128]{1,0:T(2,128)S(1)}, u32[]{:S(2)}, u32[]{:S(2)}) collective-permute-start(f32[2,128]{1,0:T(2,128)S(1)} %get-tuple-element.76), channel_id=1, source_target_pairs={{0,1},{1,0},{2,3},{3,2},{4,5},{5,4},{6,7},{7,6},{8,9},{9,8},{10,11... | collective-permute-start | bytes 3080 | tf_op jit(solution)/shard_map/ppermute | solution.py:455
  33.2 1.4 %collective-permute-start.15 = (f32[2,128]{1,0:T(2,128)S(1)}, f32[2,128]{1,0:T(2,128)S(1)}, u32[]{:S(2)}, u32[]{:S(2)}) collective-permute-start(f32[2,128]{1,0:T(2,128)S(1)} %get-tuple-element.78), channel_id=1, source_target_pairs={{0,3},{1,2},{2,1},{3,0},{4,8},{5,9},{6,10},{7,11},{8,4},{9,5},{10,... | collective-permute-start | bytes 3080 | tf_op jit(solution)/shard_map/ppermute | solution.py:455
  34.6 0.3 shard_map.167.local
  35.2 2.5 %collective-permute-done.15.a3 = f32[2,128]{1,0:T(2,128)S(1)} collective-permute-done((f32[2,128]{1,0:T(2,128)S(1)}, f32[2,128]{1,0:T(2,128)S(1)}, u32[]{:S(2)}, u32[]{:S(2)}) %collective-permute-start.15) | collective-permute-done | bytes 1056 | tf_op jit(solution)/shard_map/ppermute | solution.py:455
  37.7 0.3 shard_map.168
  38.0 1.9 %collective-permute-start.17 = (f32[2,128]{1,0:T(2,128)S(1)}, f32[2,128]{1,0:T(2,128)S(1)}, u32[]{:S(2)}, u32[]{:S(2)}) collective-permute-start(f32[2,128]{1,0:T(2,128)S(1)} %get-tuple-element.81), channel_id=1, source_target_pairs={{0,1},{1,0},{2,3},{3,2},{4,5},{5,4},{6,7},{7,6},{8,9},{9,8},{10,11... | collective-permute-start | bytes 3080 | tf_op jit(solution)/shard_map/ppermute | solution.py:455
  39.9 1.6 %collective-permute-start.19 = (f32[2,128]{1,0:T(2,128)S(1)}, f32[2,128]{1,0:T(2,128)S(1)}, u32[]{:S(2)}, u32[]{:S(2)}) collective-permute-start(f32[2,128]{1,0:T(2,128)S(1)} %get-tuple-element.83), channel_id=1, source_target_pairs={{0,3},{1,2},{2,1},{3,0},{4,8},{5,9},{6,10},{7,11},{8,4},{9,5},{10,... | collective-permute-start | bytes 3080 | tf_op jit(solution)/shard_map/ppermute | solution.py:455
  41.5 0.3 shard_map.169.local
  41.9 2.5 %collective-permute-done.19.a3 = f32[2,128]{1,0:T(2,128)S(1)} collective-permute-done((f32[2,128]{1,0:T(2,128)S(1)}, f32[2,128]{1,0:T(2,128)S(1)}, u32[]{:S(2)}, u32[]{:S(2)}) %collective-permute-start.19) | collective-permute-done | bytes 1056 | tf_op jit(solution)/shard_map/ppermute | solution.py:455
  44.4 0.7 %shard_map.170 = (f32[8,128]{1,0:T(8,128)S(1)}, f32[8,128]{1,0:T(8,128)S(1)}, f32[32,1,1152]{2,1,0:T(1,128)S(1)}) custom-call(s32[8,128]{1,0:T(8,128)S(1)} %get-tuple-element.46.places, f32[2,128]{1,0:T(2,128)S(1)} %collective-permute-done.16.a0, f32[2,128]{1,0:T(2,128)S(1)} %collective-permute-done.17.a1, f32[2,128]{1,0:T(2,128)S(1)} %collective-permute-done.18.a2, ...), custom_call_target="tpu_custom_call" | custom-call | flops 1000000 | bytes 1000000 | tf_op jit(solution)/shard_map/pallas_call | solution.py:29
  45.1 10.4 %all_to_all.5.packets = f32[32,1,1152]{2,1,0:T(1,128)S(1)} all-to-all(f32[32,1,1152]{2,1,0:T(1,128)S(1)} %get-tuple-element.85), channel_id=1, replica_groups=mesh['dom'=8,'sub'=4] {'dom','sub'}, dimensions={0} | all-to-all | bytes 294912 | tf_op jit(solution)/shard_map/all_to_all | solution.py:463
  55.5 1.4 %shard_map.171 = (f32[8,128]{1,0:T(8,128)}, f32[8,128]{1,0:T(8,128)}) custom-call(s32[8]{0:T(128)S(1)} %stack.35.where, f32[32,1,1152]{2,1,0:T(1,128)S(1)} %all_to_all.5.packets, s32[8,128]{1,0:T(8,128)S(1)} %get-tuple-element.46.places, f32[8,128]{1,0:T(8,128)S(1)} %get-tuple-element.86.image, f32[8,128]{1,0:T(8,128)S(1)} %get-tuple-element.73.vector.guess, ...), custom_call_target="tpu_custom_call" | custom-call | flops 1000000 | bytes 1000000 | tf_op jit(solution)/shard_map/pallas_call | solution.py:29
  (34 shorter events, 0.6 us)
Async XLA Ops:
  0.6 8.9 %copy-start.1 = (bf16[2,256,256]{2,1,0:T(8,128)(2,1)S(1)}, bf16[2,256,256]{2,1,0:T(8,128)(2,1)}, u32[]{:S(2)}) copy-start(bf16[2,256,256]{2,1,0:T(8,128)(2,1)} %w_self.3) | copy-start | bytes 786436
  0.6 8.9 %copy-start = (f32[1,24,128,128]{3,2,1,0:T(8,128)S(1)}, f32[1,24,128,128]{3,2,1,0:T(8,128)}, u32[]{:S(2)}) copy-start(f32[1,24,128,128]{3,2,1,0:T(8,128)} %tiles.1) | copy-start | bytes 4718596
  2.8 10.9 %copy-start.2 = (bf16[2,256,256]{2,1,0:T(8,128)(2,1)S(1)}, bf16[2,256,256]{2,1,0:T(8,128)(2,1)}, u32[]{:S(2)}) copy-start(bf16[2,256,256]{2,1,0:T(8,128)(2,1)} %w_out.3) | copy-start | bytes 786436
  2.8 10.9 %copy-start.3 = (bf16[2,256,256]{2,1,0:T(8,128)(2,1)S(1)}, bf16[2,256,256]{2,1,0:T(8,128)(2,1)}, u32[]{:S(2)}) copy-start(bf16[2,256,256]{2,1,0:T(8,128)(2,1)} %w_neighbour.3) | copy-start | bytes 786436
  2.8 9.0 %collective-permute-start = (bf16[256,256]{1,0:T(8,128)(2,1)S(1)}, bf16[256,256]{1,0:T(8,128)(2,1)S(1)}, u32[]{:S(2)}, u32[]{:S(2)}) collective-permute-start(bf16[256,256]{1,0:T(8,128)(2,1)S(1)} %get-tuple-element.47), channel_id=1, source_target_pairs={{0,4},{1,2},{2,1},{3,7},{4,0},{5,6},{6,5},{7,3},{8,12},{9,10},{10,... | collective-permute-start | bytes 393224 | tf_op jit(solution)/shard_map/ppermute | solution.py:455
  4.6 8.7 %collective-permute-start.1 = (bf16[256,256]{1,0:T(8,128)(2,1)S(1)}, bf16[256,256]{1,0:T(8,128)(2,1)S(1)}, u32[]{:S(2)}, u32[]{:S(2)}) collective-permute-start(bf16[256,256]{1,0:T(8,128)(2,1)S(1)} %get-tuple-element.49), channel_id=1, source_target_pairs={{0,1},{1,0},{2,3},{3,2},{4,5},{5,4},{6,7},{7,6},{8,9},{9,8},{10,11... | collective-permute-start | bytes 393224 | tf_op jit(solution)/shard_map/ppermute | solution.py:455
  8.7 4.6 %collective-permute-start.2 = (bf16[256,256]{1,0:T(8,128)(2,1)S(1)}, bf16[256,256]{1,0:T(8,128)(2,1)S(1)}, u32[]{:S(2)}, u32[]{:S(2)}) collective-permute-start(bf16[256,256]{1,0:T(8,128)(2,1)S(1)} %get-tuple-element.50), channel_id=1, source_target_pairs={{0,4},{1,5},{2,6},{3,7},{4,0},{5,1},{6,2},{7,3},{8,12},{9,13},{10,... | collective-permute-start | bytes 393224 | tf_op jit(solution)/shard_map/ppermute | solution.py:455
  8.7 5.0 %collective-permute-start.3 = (bf16[256,256]{1,0:T(8,128)(2,1)S(1)}, bf16[256,256]{1,0:T(8,128)(2,1)S(1)}, u32[]{:S(2)}, u32[]{:S(2)}) collective-permute-start(bf16[256,256]{1,0:T(8,128)(2,1)S(1)} %get-tuple-element.51), channel_id=1, source_target_pairs={{0,2},{1,3},{2,0},{3,1},{4,8},{5,9},{6,10},{7,11},{8,4},{9,5},{10,... | collective-permute-start | bytes 393224 | tf_op jit(solution)/shard_map/ppermute | solution.py:455
  15.3 4.0 %collective-permute-start.4 = (bf16[256,256]{1,0:T(8,128)(2,1)S(1)}, bf16[256,256]{1,0:T(8,128)(2,1)S(1)}, u32[]{:S(2)}, u32[]{:S(2)}) collective-permute-start(bf16[256,256]{1,0:T(8,128)(2,1)S(1)} %get-tuple-element.58), channel_id=1, source_target_pairs={{0,4},{1,2},{2,1},{3,7},{4,0},{5,6},{6,5},{7,3},{8,12},{9,10},{10,... | collective-permute-start | bytes 393224 | tf_op jit(solution)/shard_map/ppermute | solution.py:455
  16.0 7.2 %collective-permute-start.5 = (bf16[256,256]{1,0:T(8,128)(2,1)S(1)}, bf16[256,256]{1,0:T(8,128)(2,1)S(1)}, u32[]{:S(2)}, u32[]{:S(2)}) collective-permute-start(bf16[256,256]{1,0:T(8,128)(2,1)S(1)} %get-tuple-element.60), channel_id=1, source_target_pairs={{0,1},{1,0},{2,3},{3,2},{4,5},{5,4},{6,7},{7,6},{8,9},{9,8},{10,11... | collective-permute-start | bytes 393224 | tf_op jit(solution)/shard_map/ppermute | solution.py:455
  18.0 5.2 %collective-permute-start.6 = (bf16[256,256]{1,0:T(8,128)(2,1)S(1)}, bf16[256,256]{1,0:T(8,128)(2,1)S(1)}, u32[]{:S(2)}, u32[]{:S(2)}) collective-permute-start(bf16[256,256]{1,0:T(8,128)(2,1)S(1)} %get-tuple-element.61), channel_id=1, source_target_pairs={{0,4},{1,5},{2,6},{3,7},{4,0},{5,1},{6,2},{7,3},{8,12},{9,13},{10,... | collective-permute-start | bytes 393224 | tf_op jit(solution)/shard_map/ppermute | solution.py:455
  18.0 5.2 %collective-permute-start.7 = (bf16[256,256]{1,0:T(8,128)(2,1)S(1)}, bf16[256,256]{1,0:T(8,128)(2,1)S(1)}, u32[]{:S(2)}, u32[]{:S(2)}) collective-permute-start(bf16[256,256]{1,0:T(8,128)(2,1)S(1)} %get-tuple-element.62), channel_id=1, source_target_pairs={{0,2},{1,3},{2,0},{3,1},{4,8},{5,9},{6,10},{7,11},{8,4},{9,5},{10,... | collective-permute-start | bytes 393224 | tf_op jit(solution)/shard_map/ppermute | solution.py:455
  24.6 3.8 %collective-permute-start.8 = (f32[2,128]{1,0:T(2,128)S(1)}, f32[2,128]{1,0:T(2,128)S(1)}, u32[]{:S(2)}, u32[]{:S(2)}) collective-permute-start(f32[2,128]{1,0:T(2,128)S(1)} %get-tuple-element.68), channel_id=1, source_target_pairs={{0,4},{1,2},{2,1},{3,7},{4,0},{5,6},{6,5},{7,3},{8,12},{9,10},{10,... | collective-permute-start | bytes 3080 | tf_op jit(solution)/shard_map/ppermute | solution.py:455
  24.7 3.8 %collective-permute-start.9 = (f32[2,128]{1,0:T(2,128)S(1)}, f32[2,128]{1,0:T(2,128)S(1)}, u32[]{:S(2)}, u32[]{:S(2)}) collective-permute-start(f32[2,128]{1,0:T(2,128)S(1)} %get-tuple-element.69), channel_id=1, source_target_pairs={{0,1},{1,0},{2,3},{3,2},{4,5},{5,4},{6,7},{7,6},{8,9},{9,8},{10,11... | collective-permute-start | bytes 3080 | tf_op jit(solution)/shard_map/ppermute | solution.py:455
  26.8 1.7 %collective-permute-start.10 = (f32[2,128]{1,0:T(2,128)S(1)}, f32[2,128]{1,0:T(2,128)S(1)}, u32[]{:S(2)}, u32[]{:S(2)}) collective-permute-start(f32[2,128]{1,0:T(2,128)S(1)} %get-tuple-element.70), channel_id=1, source_target_pairs={{0,4},{1,5},{2,6},{3,7},{4,0},{5,1},{6,2},{7,3},{8,12},{9,13},{10,... | collective-permute-start | bytes 3080 | tf_op jit(solution)/shard_map/ppermute | solution.py:455
  26.8 4.5 %collective-permute-start.11 = (f32[2,128]{1,0:T(2,128)S(1)}, f32[2,128]{1,0:T(2,128)S(1)}, u32[]{:S(2)}, u32[]{:S(2)}) collective-permute-start(f32[2,128]{1,0:T(2,128)S(1)} %get-tuple-element.71), channel_id=1, source_target_pairs={{0,3},{1,2},{2,1},{3,0},{4,8},{5,9},{6,10},{7,11},{8,4},{9,5},{10,... | collective-permute-start | bytes 3080 | tf_op jit(solution)/shard_map/ppermute | solution.py:455
  28.1 3.1 %copy-start.4 = (f32[1024]{0:T(1024)S(1)}, f32[1024]{0:T(1024)}, u32[]{:S(2)}) copy-start(f32[1024]{0:T(1024)} %param.23) | copy-start | bytes 12292
  31.5 3.5 %collective-permute-start.12 = (f32[2,128]{1,0:T(2,128)S(1)}, f32[2,128]{1,0:T(2,128)S(1)}, u32[]{:S(2)}, u32[]{:S(2)}) collective-permute-start(f32[2,128]{1,0:T(2,128)S(1)} %get-tuple-element.75), channel_id=1, source_target_pairs={{0,4},{1,2},{2,1},{3,7},{4,0},{5,6},{6,5},{7,3},{8,12},{9,10},{10,... | collective-permute-start | bytes 3080 | tf_op jit(solution)/shard_map/ppermute | solution.py:455
  31.6 3.6 %collective-permute-start.13 = (f32[2,128]{1,0:T(2,128)S(1)}, f32[2,128]{1,0:T(2,128)S(1)}, u32[]{:S(2)}, u32[]{:S(2)}) collective-permute-start(f32[2,128]{1,0:T(2,128)S(1)} %get-tuple-element.76), channel_id=1, source_target_pairs={{0,1},{1,0},{2,3},{3,2},{4,5},{5,4},{6,7},{7,6},{8,9},{9,8},{10,11... | collective-permute-start | bytes 3080 | tf_op jit(solution)/shard_map/ppermute | solution.py:455
  33.2 2.0 %collective-permute-start.14 = (f32[2,128]{1,0:T(2,128)S(1)}, f32[2,128]{1,0:T(2,128)S(1)}, u32[]{:S(2)}, u32[]{:S(2)}) collective-permute-start(f32[2,128]{1,0:T(2,128)S(1)} %get-tuple-element.77), channel_id=1, source_target_pairs={{0,4},{1,5},{2,6},{3,7},{4,0},{5,1},{6,2},{7,3},{8,12},{9,13},{10,... | collective-permute-start | bytes 3080 | tf_op jit(solution)/shard_map/ppermute | solution.py:455
  33.2 4.5 %collective-permute-start.15 = (f32[2,128]{1,0:T(2,128)S(1)}, f32[2,128]{1,0:T(2,128)S(1)}, u32[]{:S(2)}, u32[]{:S(2)}) collective-permute-start(f32[2,128]{1,0:T(2,128)S(1)} %get-tuple-element.78), channel_id=1, source_target_pairs={{0,3},{1,2},{2,1},{3,0},{4,8},{5,9},{6,10},{7,11},{8,4},{9,5},{10,... | collective-permute-start | bytes 3080 | tf_op jit(solution)/shard_map/ppermute | solution.py:455
  38.0 3.9 %collective-permute-start.16 = (f32[2,128]{1,0:T(2,128)S(1)}, f32[2,128]{1,0:T(2,128)S(1)}, u32[]{:S(2)}, u32[]{:S(2)}) collective-permute-start(f32[2,128]{1,0:T(2,128)S(1)} %get-tuple-element.80), channel_id=1, source_target_pairs={{0,4},{1,2},{2,1},{3,7},{4,0},{5,6},{6,5},{7,3},{8,12},{9,10},{10,... | collective-permute-start | bytes 3080 | tf_op jit(solution)/shard_map/ppermute | solution.py:455
  38.0 3.9 %collective-permute-start.17 = (f32[2,128]{1,0:T(2,128)S(1)}, f32[2,128]{1,0:T(2,128)S(1)}, u32[]{:S(2)}, u32[]{:S(2)}) collective-permute-start(f32[2,128]{1,0:T(2,128)S(1)} %get-tuple-element.81), channel_id=1, source_target_pairs={{0,1},{1,0},{2,3},{3,2},{4,5},{5,4},{6,7},{7,6},{8,9},{9,8},{10,11... | collective-permute-start | bytes 3080 | tf_op jit(solution)/shard_map/ppermute | solution.py:455
  39.9 2.0 %collective-permute-start.18 = (f32[2,128]{1,0:T(2,128)S(1)}, f32[2,128]{1,0:T(2,128)S(1)}, u32[]{:S(2)}, u32[]{:S(2)}) collective-permute-start(f32[2,128]{1,0:T(2,128)S(1)} %get-tuple-element.82), channel_id=1, source_target_pairs={{0,4},{1,5},{2,6},{3,7},{4,0},{5,1},{6,2},{7,3},{8,12},{9,13},{10,... | collective-permute-start | bytes 3080 | tf_op jit(solution)/shard_map/ppermute | solution.py:455
  39.9 4.5 %collective-permute-start.19 = (f32[2,128]{1,0:T(2,128)S(1)}, f32[2,128]{1,0:T(2,128)S(1)}, u32[]{:S(2)}, u32[]{:S(2)}) collective-permute-start(f32[2,128]{1,0:T(2,128)S(1)} %get-tuple-element.83), channel_id=1, source_target_pairs={{0,3},{1,2},{2,1},{3,0},{4,8},{5,9},{6,10},{7,11},{8,4},{9,5},{10,... | collective-permute-start | bytes 3080 | tf_op jit(solution)/shard_map/ppermute | solution.py:455
